TPU v7x, 32 devices: a whole 2x2x4 slice. The times are simulated.
32 devices in a mesh: lat: 8 (over z, x), lon: 4 (over y, core).
Axes of the slice: x: 2, y: 2, z: 4, core: 2. Of those that a mesh axis runs over, the one named last changes fastest.
Arguments:
- cotangent: bfloat16 [128, 1440, 256], P('lat', 'lon'), may hold values from -6 to 6
- legendre: bfloat16 [128, 384, 192], P('lat', 'lon'), may hold values from -0.5 to 0.5
- spectral_weight: bfloat16 [256, 256], replicated, may hold values from -0.375 to 0.375
- skip_weight: bfloat16 [256, 256], replicated, may hold values from -0.375 to 0.375
Outputs:
- grad_input: bfloat16 [128, 1440, 256], P('lat', 'lon')
All inputs are finite; a program needn't handle non-finite values.
Results may differ from a plain program's by a relative error of at most 0.015.
Values may be sent and summed in bfloat16 or wider, within the bound.
A program may use at most 128 MiB of HBM per device.

v0:
```python
import math

import jax
import jax.numpy as jnp
from jax import lax
from jax.sharding import PartitionSpec as P


def swapped(value, axis, apart):
    mask = 2**apart
    pairs = [(source, source ^ mask) for source in range(lax.axis_size(axis))]
    return lax.ppermute(value, axis, pairs)


def fourier_table(count_lon, count_wave):
    longitude = lax.broadcasted_iota(jnp.int32, (count_lon, count_wave), 0)
    wavenum = lax.broadcasted_iota(jnp.int32, (count_lon, count_wave), 1)
    phases = longitude * wavenum % count_lon
    angles = phases.astype(jnp.float32) * (2.0 * math.pi / count_lon)
    norm_scale = math.sqrt(2.0 / count_lon)
    stacked = jnp.stack([norm_scale * jnp.cos(angles), -norm_scale * jnp.sin(angles)], axis=2)
    return stacked.reshape(count_lon, 2 * count_wave)


def degree_masks(wave_start, wave_count, half_deg):
    wavenum = wave_start + lax.broadcasted_iota(jnp.int32, (wave_count, half_deg), 0)
    degree = 2 * lax.broadcasted_iota(jnp.int32, (wave_count, half_deg), 1)
    parity = wavenum % 2
    return (degree + parity >= wavenum, degree + 1 - parity >= wavenum)


def mix_channels(spectral, spectral_weight):
    width = spectral.shape[-1]
    flat_values = spectral.reshape(-1, width)
    mixed_out = jnp.dot(flat_values, spectral_weight.T, preferred_element_type=jnp.float32)
    return mixed_out.astype(jnp.bfloat16).reshape(spectral.shape)


def shards(cotangent, legendre, spectral_weight, skip_weight):
    lat_rows, lon_dev, width = cotangent.shape
    lat_count = lax.axis_size("lat")
    lon_count = lax.axis_size("lon")
    count_lon = lon_dev * lon_count
    wave_dev = legendre.shape[1]
    half_deg = legendre.shape[2]
    fourier = fourier_table(count_lon, wave_dev * lon_count)
    spectra = jnp.einsum(
        "rlc,lk->rkc",
        lax.all_to_all(cotangent, "lon", split_axis=0, concat_axis=1, tiled=True).astype(
            jnp.float32
        ),
        fourier,
        precision=lax.Precision.HIGHEST,
    )
    coeffs = lax.all_to_all(
        spectra.astype(jnp.bfloat16), "lon", split_axis=1, concat_axis=0, tiled=True
    )
    coeffs = coeffs.reshape(lat_rows, wave_dev, 2, width)
    mask_even, mask_odd = degree_masks(lax.axis_index("lon") * wave_dev, wave_dev, half_deg)
    half_count = lat_count // 2
    top_bit = lat_count.bit_length() - 2
    northern = lax.axis_index("lat") < half_count
    own_mask = jnp.where(northern, mask_even, mask_odd)
    basis = jnp.where(own_mask[None], legendre, jnp.zeros_like(legendre))
    mirrored = swapped(coeffs, "lat", top_bit)
    own_wide = coeffs.astype(jnp.float32)
    mirror_wide = mirrored.astype(jnp.float32)
    combined = jnp.where(northern, own_wide + mirror_wide, mirror_wide - own_wide).astype(
        jnp.bfloat16
    )
    partial_value = jnp.einsum(
        "rmk,rmpc->kmpc", basis, combined, preferred_element_type=jnp.float32
    ).astype(jnp.bfloat16)
    deg_block = half_deg // lat_count
    received = lax.all_to_all(
        partial_value.reshape(lat_count, deg_block, wave_dev, 2, width),
        "lat",
        split_axis=0,
        concat_axis=0,
        tiled=True,
    )
    summed = jnp.stack(
        [
            jnp.sum(received[:half_count].astype(jnp.float32), 0),
            jnp.sum(received[half_count:].astype(jnp.float32), 0),
        ]
    )
    mixed_out = mix_channels(summed.astype(jnp.bfloat16), spectral_weight)
    slot_index = lax.broadcasted_iota(jnp.int32, (lat_count, 1, 1, 1, 1), 0)
    outgoing = jnp.where(slot_index < half_count, mixed_out[0][None], mixed_out[1][None])
    returned = lax.all_to_all(outgoing, "lat", split_axis=0, concat_axis=0, tiled=True).reshape(
        half_deg, wave_dev, 2, width
    )
    projected = jnp.einsum(
        "rmk,kmpc->rmpc", basis, returned, preferred_element_type=jnp.float32
    ).astype(jnp.bfloat16)
    mirrored = swapped(projected, "lat", top_bit)
    own_wide = projected.astype(jnp.float32)
    mirror_wide = mirrored.astype(jnp.float32)
    grad_coeffs = jnp.where(northern, own_wide + mirror_wide, mirror_wide - own_wide).astype(
        jnp.bfloat16
    )
    flat_coeffs = grad_coeffs.reshape(lat_rows, 2 * wave_dev, width)
    grid_part = jnp.einsum(
        "rkc,lk->rlc",
        lax.all_to_all(flat_coeffs, "lon", split_axis=0, concat_axis=1, tiled=True).astype(
            jnp.float32
        ),
        fourier,
        precision=lax.Precision.HIGHEST,
    )
    spatial = lax.all_to_all(
        grid_part.astype(jnp.bfloat16), "lon", split_axis=1, concat_axis=0, tiled=True
    )
    skip_term = jnp.dot(
        cotangent.reshape(-1, width), skip_weight.T, preferred_element_type=jnp.float32
    ).reshape(cotangent.shape)
    return (spatial.astype(jnp.float32) + skip_term).astype(jnp.bfloat16)


def solution(mesh):
    return jax.shard_map(
        shards,
        mesh=mesh,
        in_specs=(P("lat", "lon", None), P("lat", "lon", None), P(), P()),
        out_specs=P("lat", "lon", None),
        check_vma=False,
    )
```

profile of v0, /device:TPU:11, one launch (start us, length us, event | category | flops | bytes accessed | tf_op | source)
XLA Modules:
  0.0 1223.1 jit_solution(17807651746817157702)
XLA Ops:
  0.0 0.0 copy-start
  0.0 4.5 all-to-all-start
  4.5 9.3 sine_multiply_fusion
  13.7 2.4 pad_maximum_fusion.1
  16.1 8.1 copy.58
  24.2 7.2 reshape.167
  31.4 7.1 all-to-all-done
  38.4 0.0 copy-start.3
  38.4 0.2 copy.59
  38.6 2.1 copy-done.3
  40.8 7.5 fusion.26
  48.2 1.2 copy.61
  49.4 22.4 %all_to_all.70 = bf16[4,768,256]{2,0,1:T(4,128)(2,1)S(1)} all-to-all(bf16[4,768,256]{2,0,1:T(4,128)(2,1)S(1)} %copy.61), channel_id=1, replica_groups=mesh['lat'=8,'lon'=4] {'lon'}, dimensions={1} | all-to-all | bytes 3145728 | tf_op jit(solution)/shard_map/all_to_all | solution.py:55
  71.8 0.0 copy-start.4
  71.8 1.7 copy.94
  73.5 2.4 reshape.168
  75.9 2.4 collective-permute-start
  78.3 0.1 fusion.34
  78.4 0.0 copy-done.4
  78.4 0.1 select_bitcast_fusion
  78.5 67.5 %collective-permute-done = bf16[16,96,2,256]{3,0,2,1:T(8,128)(2,1)} collective-permute-done((bf16[16,96,2,256]{3,0,2,1:T(8,128)(2,1)S(1)}, bf16[16,96,2,256]{3,0,2,1:T(8,128)(2,1)}, u32[]{:S(2)}, u32[]{:S(2)}) %collective-permute-start) | collective-permute-done | bytes 1572896 | tf_op jit(solution)/shard_map/ppermute | solution.py:12
  145.9 10.3 convolution_convert_fusion.1
  156.2 16.8 %copy.64 = bf16[8,24,96,2,256]{4,1,3,2,0:T(8,128)(2,1)} copy(bf16[8,24,96,2,256]{4,1,0,3,2:T(8,128)(2,1)} %bitcast.63) | data formatting | bytes 37748736 | tf_op jit(solution)/shard_map/reshape | solution.py:76
  173.0 6.8 all-to-all-start.2
  179.8 405.2 %all-to-all-done.2 = bf16[8,24,96,2,256]{4,1,3,2,0:T(8,128)(2,1)} async-done(((bf16[8,24,96,2,256]{4,1,3,2,0:T(8,128)(2,1)}), bf16[8,24,96,2,256]{4,1,3,2,0:T(8,128)(2,1)}, u32[]{:S(2)}, u32[]{:S(2)}) %all-to-all-start.2) | async-done | bytes 18874400 | tf_op jit(solution)/shard_map/all_to_all | solution.py:75
  585.0 9.5 slice_reduce_fusion.1
  594.5 2.6 pad_maximum_fusion
  597.0 9.6 copy.67
  606.7 8.1 convert_element_type.99
  614.7 0.0 copy-done
  614.7 3.8 convolution_convert_fusion
  618.5 1.7 fusion.36
  620.2 2.3 broadcast_in_dim.43
  622.5 4.2 copy.68
  626.7 6.2 broadcast_in_dim.45
  632.9 4.2 copy.69
  637.1 2.6 broadcast_select_fusion
  639.7 411.2 %all_to_all.71 = bf16[8,24,96,2,256]{4,1,3,2,0:T(8,128)(2,1)} all-to-all(bf16[8,24,96,2,256]{4,1,3,2,0:T(8,128)(2,1)S(1)} %broadcast_select_fusion), channel_id=1, replica_groups=mesh['lat'=8,'lon'=4] {'lat'}, dimensions={0} | all-to-all | bytes 37748736 | tf_op jit(solution)/shard_map/all_to_all | solution.py:91
  1050.9 10.0 copy.70
  1060.9 2.6 fusion.25
  1063.6 3.0 collective-permute-start.1
  1066.6 66.9 %collective-permute-done.1 = bf16[16,96,2,256]{3,0,2,1:T(8,128)(2,1)S(1)} collective-permute-done((bf16[16,96,2,256]{3,0,2,1:T(8,128)(2,1)S(1)}, bf16[16,96,2,256]{3,0,2,1:T(8,128)(2,1)S(1)}, u32[]{:S(2)}, u32[]{:S(2)}) %collective-permute-start.1) | collective-permute-done | bytes 1572896 | tf_op jit(solution)/shard_map/ppermute | solution.py:12
  1133.5 0.0 slice-start
  1133.5 0.7 fusion.14
  1134.2 0.0 slice-start.1
  1134.2 0.5 copy.72
  1134.7 22.4 %all_to_all.72 = bf16[16,192,256]{2,1,0:T(8,128)(2,1)S(1)} all-to-all(bf16[16,192,256]{2,1,0:T(8,128)(2,1)S(1)} %copy.72), channel_id=1, replica_groups=mesh['lat'=8,'lon'=4] {'lon'}, dimensions={0} | all-to-all | bytes 3145728 | tf_op jit(solution)/shard_map/all_to_all | solution.py:106
  1157.1 0.1 copy.73
  1157.2 0.0 slice-done
  1157.2 0.0 slice-done.1
  1157.3 7.9 fusion.8
  1165.2 15.0 %copy.75 = bf16[4,1440,256]{2,0,1:T(4,128)(2,1)S(1)} copy(bf16[4,1440,256]{2,1,0:T(8,128)(2,1)S(1)} %fusion.8) | data formatting | bytes 5898240 | tf_op jit(solution)/shard_map/convert_element_type | solution.py:113
  1180.2 37.6 %all_to_all.73 = bf16[4,1440,256]{2,0,1:T(4,128)(2,1)S(1)} all-to-all(bf16[4,1440,256]{2,0,1:T(4,128)(2,1)S(1)} %copy.75), channel_id=1, replica_groups=mesh['lat'=8,'lon'=4] {'lon'}, dimensions={1} | all-to-all | bytes 5898240 | tf_op jit(solution)/shard_map/all_to_all | solution.py:112
  1217.8 0.0 copy-start.2
  1217.8 0.0 copy-start.5
  1217.8 0.5 copy.76
  1218.4 1.3 copy-done.2
  1219.7 0.0 copy-done.5
  1219.7 0.0 copy-start.1
  1219.7 3.0 fusion
  1222.6 0.0 copy-done.1
  (6 shorter events, 0.0 us)
Async XLA Ops:
  0.0 614.7 %copy-start = (bf16[256,256]{1,0:T(8,128)(2,1)S(1)}, bf16[256,256]{1,0:T(8,128)(2,1)}, u32[]{:S(2)}) copy-start(bf16[256,256]{1,0:T(8,128)(2,1)} %param.6) | copy-start | bytes 393220
  0.0 38.4 %all-to-all-start = ((bf16[16,360,256]{2,1,0:T(8,128)(2,1)}), bf16[16,360,256]{2,1,0:T(8,128)(2,1)S(1)}, u32[]{:S(2)}, u32[]{:S(2)}) async-start(bf16[16,360,256]{2,1,0:T(8,128)(2,1)} %param.4), calls=%async_computation | async-start | bytes 5898240 | tf_op jit(solution)/shard_map/all_to_all | solution.py:49
  38.4 2.3 copy-start.3
  71.8 6.6 copy-start.4
  75.9 70.1 %collective-permute-start = (bf16[16,96,2,256]{3,0,2,1:T(8,128)(2,1)S(1)}, bf16[16,96,2,256]{3,0,2,1:T(8,128)(2,1)}, u32[]{:S(2)}, u32[]{:S(2)}) collective-permute-start(bf16[16,96,2,256]{3,0,2,1:T(8,128)(2,1)S(1)} %reshape.168), channel_id=1, source_target_pairs={{0,16},{4,20},{8,24},{12,28},{16,0},{20,4},{24,8},{28,12},{1,17},{... | collective-permute-start | bytes 4718600 | tf_op jit(solution)/shard_map/ppermute | solution.py:12
  173.0 412.0 %all-to-all-start.2 = ((bf16[8,24,96,2,256]{4,1,3,2,0:T(8,128)(2,1)}), bf16[8,24,96,2,256]{4,1,3,2,0:T(8,128)(2,1)}, u32[]{:S(2)}, u32[]{:S(2)}) async-start(bf16[8,24,96,2,256]{4,1,3,2,0:T(8,128)(2,1)} %copy.64), calls=%async_computation.2 | async-start | bytes 37748736 | tf_op jit(solution)/shard_map/all_to_all | solution.py:75
  1063.6 69.9 %collective-permute-start.1 = (bf16[16,96,2,256]{3,0,2,1:T(8,128)(2,1)S(1)}, bf16[16,96,2,256]{3,0,2,1:T(8,128)(2,1)S(1)}, u32[]{:S(2)}, u32[]{:S(2)}) collective-permute-start(bf16[16,96,2,256]{3,0,2,1:T(8,128)(2,1)S(1)} %fusion.25), channel_id=1, source_target_pairs={{0,16},{4,20},{8,24},{12,28},{16,0},{20,4},{24,8},{28,12},{1,17},{... | collective-permute-start | bytes 4718600 | tf_op jit(solution)/shard_map/ppermute | solution.py:12
  1133.5 23.8 %slice-start = ((s8[4718592]{0:T(1024)(128)(4,1)}), s8[4194304]{0:T(1024)(128)(4,1)S(1)}, s32[]{:S(2)}) async-start(s8[4718592]{0:T(1024)(128)(4,1)} %bitcast.73), calls=%async_computation.6 | async-start | bytes 8388608
  1134.2 23.0 %slice-start.1 = ((s8[4718592]{0:T(1024)(128)(4,1)}), s8[524288]{0:T(1024)(128)(4,1)S(1)}, s32[]{:S(2)}) async-start(s8[4718592]{0:T(1024)(128)(4,1)} %bitcast.73), calls=%async_computation.7 | async-start | bytes 1048576
  1217.8 1.8 copy-start.2
  1217.8 1.8 copy-start.5
  1219.7 3.0 copy-start.1
where the time goes:
time: 1240 us; the launch traced here: 1220 us
  waiting for transfers between devices  547 us (44%)
  blocking collectives  494 us (40%)
  local copies, waits for them, and re-layouts  103 us (8%)
  matrix products  35 us (3%)
  other arithmetic  27.2 us (2%)
  starting transfers between devices  16.6 us (1%)
    all_to_all x1, blocking collectives, shards(): lax.all_to_all(outgoing, 'lat', split_axis=0, concat_axis=0, tiled=True)  411 us
    all_to_all x1, waiting for transfers between devices, shards(): lax.all_to_all(partial_value.reshape(lat_count, deg_block, wave_dev, 2, w...  405 us
    ppermute x2, waiting for transfers between devices, swapped(): return lax.ppermute(value, axis, pairs)  134 us
    all_to_all x1, blocking collectives, shards(): lax.all_to_all(grid_part.astype(jnp.bfloat16), 'lon', split_axis=1, conca...  37.6 us
  transfers between devices with their start and end apart: 4, of which 4 were waited for; matrix products, arithmetic and copies ran while one was open for 2% of the time, Pallas kernels for 0%

commit v1 on v0

v1 whole, which is shorter than its diff:
```python
import functools
import math

import jax
import jax.numpy as jnp
import numpy as np
from jax import lax
from jax.sharding import PartitionSpec as P

BOTH = ("lat", "lon")


def fourier_table(count_lon, count_wave, lat_count, lon_count, wave_each):
    wave_dev = count_wave // lon_count
    place = np.arange(lat_count * wave_each).reshape(lat_count, 1, wave_each)
    wavenum = place + wave_dev * np.arange(lon_count).reshape(1, lon_count, 1)
    real = np.broadcast_to(place < wave_dev, wavenum.shape)
    phases = wavenum[..., None] * np.arange(count_lon) % count_lon
    angles = phases * (2.0 * math.pi / count_lon)
    norm_scale = math.sqrt(2.0 / count_lon)
    table = np.stack([norm_scale * np.cos(angles), -norm_scale * np.sin(angles)], axis=2)
    table = np.where(real[:, :, None, :, None], table, 0.0)
    return table.reshape(-1, count_lon).astype(jnp.bfloat16)


def shards(table, cotangent, legendre, spectral_weight, skip_weight):
    lat_rows, lon_dev, width = cotangent.shape
    lat_count = lax.axis_size("lat")
    lon_count = lax.axis_size("lon")
    wave_dev, half_deg = legendre.shape[1:]
    wave_each = -(-wave_dev // lat_count)
    count_lat = lat_rows * lat_count
    half_rows = count_lat // 2
    fourier = jnp.asarray(table)

    rows = lax.all_to_all(cotangent, "lon", split_axis=0, concat_axis=1, tiled=True)
    padded = jnp.pad(legendre, ((0, 0), (0, wave_each * lat_count - wave_dev), (0, 0)))
    basis = lax.all_to_all(padded, "lat", split_axis=1, concat_axis=0, tiled=True)
    spectra = jnp.einsum(
        "kl,rlc->rkc", fourier, rows, preferred_element_type=jnp.float32
    ).astype(jnp.bfloat16)
    coeffs = lax.all_to_all(spectra, BOTH, split_axis=1, concat_axis=0, tiled=True)
    coeffs = coeffs.reshape(2, half_rows, 2, wave_each, width)

    wave_start = lax.axis_index("lon") * wave_dev + lax.axis_index("lat") * wave_each
    wavenum = wave_start + lax.broadcasted_iota(jnp.int32, (2, 1, wave_each, half_deg), 2)
    degree = 2 * lax.broadcasted_iota(jnp.int32, (2, 1, wave_each, half_deg), 3)
    half = lax.broadcasted_iota(jnp.int32, (2, 1, wave_each, half_deg), 0)
    parity = wavenum % 2
    degree = degree + jnp.where(half == 0, parity, 1 - parity)
    basis = basis.reshape(2, half_rows, wave_each, half_deg)
    basis = jnp.where(degree >= wavenum, basis, jnp.zeros_like(basis))

    wide = coeffs.astype(jnp.float32)
    combined = jnp.stack([wide[0] + wide[1], wide[0] - wide[1]]).astype(jnp.bfloat16)
    sums = jnp.einsum(
        "qrmk,qrpmc->qmkpc", basis, combined, preferred_element_type=jnp.float32
    ).astype(jnp.bfloat16)
    mixed = jnp.einsum(
        "qmkpc,dc->qmkpd", sums, spectral_weight, preferred_element_type=jnp.float32
    ).astype(jnp.bfloat16)
    projected = jnp.einsum(
        "qrmk,qmkpc->qrpmc", basis, mixed, preferred_element_type=jnp.float32
    ).astype(jnp.bfloat16).astype(jnp.float32)
    grads = jnp.stack([projected[0] + projected[1], projected[0] - projected[1]])
    grads = grads.astype(jnp.bfloat16).reshape(count_lat, 2 * wave_each, width)
    grads = lax.all_to_all(grads, BOTH, split_axis=0, concat_axis=1, tiled=True)
    grid_part = jnp.einsum(
        "kl,rkc->rlc", fourier, grads, preferred_element_type=jnp.float32
    ).astype(jnp.bfloat16)
    spatial = lax.all_to_all(grid_part, "lon", split_axis=1, concat_axis=0, tiled=True)
    skip_term = jnp.dot(
        cotangent.reshape(-1, width), skip_weight.T, preferred_element_type=jnp.float32
    ).reshape(cotangent.shape)
    return (spatial.astype(jnp.float32) + skip_term).astype(jnp.bfloat16)


def solution(mesh):
    lat_count, lon_count = mesh.shape["lat"], mesh.shape["lon"]

    def whole(cotangent, legendre, spectral_weight, skip_weight):
        count_wave = legendre.shape[1]
        wave_each = -(-(count_wave // lon_count) // lat_count)
        table = fourier_table(cotangent.shape[1], count_wave, lat_count, lon_count, wave_each)
        return jax.shard_map(
            functools.partial(shards, table),
            mesh=mesh,
            in_specs=(P("lat", "lon", None), P("lat", "lon", None), P(), P()),
            out_specs=P("lat", "lon", None),
            check_vma=False,
        )(cotangent, legendre, spectral_weight, skip_weight)

    return whole
```

time: 1240 us -> 221 us (0.18); the launches traced: 1220 us -> 218 us
  waiting for transfers between devices: 547 us -> 75.5 us
  blocking collectives: 494 us -> 80.2 us
  local copies, waits for them, and re-layouts: 103 us -> 27.5 us
  other arithmetic: 27.2 us -> 2.52 us
  matrix products: 35 us -> 15.8 us
    all_to_all x4 -> x2, blocking collectives: 494 us -> 80.2 us  [the longest x1 42.6 us: shards(): grads = lax.all_to_all(grads, BOTH, split_axis=0, concat_axis=1, tiled=True)]
    all_to_all x1 -> x2, waiting for transfers between devices: 405 us -> 44 us  [the longest x1 33.1 us: shards(): lax.all_to_all(spectra, BOTH, split_axis=1, concat_axis=0, tiled=True)]
    ppermute x2 -> x0, waiting for transfers between devices: 134 us -> none  [swapped(): return lax.ppermute(value, axis, pairs)]
    reshape x4 -> x0, local copies, waits for them, and re-layouts: 26.9 us -> none  [the longest x1 16.8 us: shards(): partial_value.reshape(lat_count, deg_block, wave_dev, 2, width)]
    all_to_all x1, waiting for transfers between devices: 7.06 us -> 31.5 us  [shards(): lax.all_to_all(cotangent, 'lon', split_axis=0, concat_axis=1, tiled=True)]
    dot_general x5 -> x4, matrix products: 32.1 us -> 12.9 us  [the longest x1 4.43 us: shards(): jnp.einsum('qmkpc,dc->qmkpd', sums, spectral_weight, preferred_element_ty...]
    another operation x2 -> x1, local copies, waits for them, and re-layouts: 17.7 us -> 0.1 us  [shards(): jnp.stack([projected[0] + projected[1], projected[0] - projected[1]])]
    broadcast_in_dim x4 -> x0, local copies, waits for them, and re-layouts: 16.9 us -> none  [shards(): jnp.where(slot_index < half_count, mixed_out[0][None], mixed_out[1][None])]
  transfers between devices with their start and end apart: 4 -> 3, of which waited for: 4 -> 3; matrix products, arithmetic and copies ran while one was open for 2% -> 4% of each run, Pallas kernels for 0% -> 0%
where the time goes in v1:
time: 221 us; the launch traced here: 218 us
  blocking collectives  80.2 us (36%)
  waiting for transfers between devices  75.5 us (34%)
  local copies, waits for them, and re-layouts  27.5 us (12%)
  starting transfers between devices  16.2 us (7%)
  matrix products  15.8 us (7%)
  other arithmetic  2.52 us (1%)
    all_to_all x1, blocking collectives, shards(): grads = lax.all_to_all(grads, BOTH, split_axis=0, concat_axis=1, tiled=True)  42.6 us
    all_to_all x1, blocking collectives, shards(): lax.all_to_all(grid_part, 'lon', split_axis=1, concat_axis=0, tiled=True)  37.6 us
    all_to_all x1, waiting for transfers between devices, shards(): lax.all_to_all(spectra, BOTH, split_axis=1, concat_axis=0, tiled=True)  33.1 us
    all_to_all x1, waiting for transfers between devices, shards(): lax.all_to_all(cotangent, 'lon', split_axis=0, concat_axis=1, tiled=True)  31.5 us
    convert_element_type x1, local copies, waits for them, and re-layouts, shards(): grid_part = jnp.einsum('kl,rkc->rlc', fourier, grads, preferred_element_t...  15 us
    all_to_all x1, waiting for transfers between devices, shards(): lax.all_to_all(padded, 'lat', split_axis=1, concat_axis=0, tiled=True)  10.9 us
    unnamed x11, local copies, waits for them, and re-layouts  6.74 us
    all_to_all x1, starting transfers between devices, shards(): lax.all_to_all(spectra, BOTH, split_axis=1, concat_axis=0, tiled=True)  6.05 us
  transfers between devices with their start and end apart: 3, of which 3 were waited for; matrix products, arithmetic and copies ran while one was open for 4% of the time, Pallas kernels for 0%

profile of v1, /device:TPU:11, one launch (start us, length us, event | category | flops | bytes accessed | tf_op | source)
XLA Modules:
  0.0 217.8 jit_solution(6837881333606668595)
XLA Ops:
  0.0 0.0 copy-start
  0.0 4.5 %all-to-all-start.1 = ((bf16[16,360,256]{2,1,0:T(8,128)(2,1)}), bf16[16,360,256]{2,1,0:T(8,128)(2,1)S(1)}, u32[]{:S(2)}, u32[]{:S(2)}) async-start(bf16[16,360,256]{2,1,0:T(8,128)(2,1)} %param.5), calls=%async_computation.1 | async-start | bytes 5898240 | tf_op jit(solution)/shard_map/all_to_all | solution.py:36
  4.5 2.5 %copy.17 = bf16[16,96,192]{2,0,1:T(8,128)(2,1)} copy(bf16[16,96,192]{2,1,0:T(8,128)(2,1)} %param.6) | data formatting | bytes 1179648 | tf_op args[1]
  6.9 31.5 %all-to-all-done.1 = bf16[16,360,256]{2,1,0:T(8,128)(2,1)S(1)} async-done(((bf16[16,360,256]{2,1,0:T(8,128)(2,1)}), bf16[16,360,256]{2,1,0:T(8,128)(2,1)S(1)}, u32[]{:S(2)}, u32[]{:S(2)}) %all-to-all-start.1) | async-done | bytes 2949152 | tf_op jit(solution)/shard_map/all_to_all | solution.py:36
  38.4 5.7 %all-to-all-start = ((bf16[16,96,192]{2,0,1:T(8,128)(2,1)}), bf16[16,96,192]{2,0,1:T(8,128)(2,1)}, u32[]{:S(2)}, u32[]{:S(2)}) async-start(bf16[16,96,192]{2,0,1:T(8,128)(2,1)} %copy.17), calls=%async_computation | async-start | bytes 1572864 | tf_op jit(solution)/shard_map/all_to_all | solution.py:38
  44.1 0.0 copy-start.3
  44.1 0.2 copy.19
  44.3 1.4 copy-done.3
  45.7 2.6 %fusion.15 = bf16[4,768,256]{2,1,0:T(8,128)(2,1)S(1)} fusion(bf16[768,1440,1]{0,1,2:T(8,128)(2,1)S(1)} %copy-done.3, bf16[4,1440,256]{2,1,0:T(8,128)(2,1)S(1)} %bitcast.63), kind=kOutput, calls=%fused_computation.20 | convolution fusion | flops 2265710592 | bytes 6733824 | tf_op jit(solution)/shard_map/kl,rlc->rkc/dot_general | solution.py:39
  48.4 2.4 %copy.20 = bf16[4,768,256]{2,0,1:T(4,128)(2,1)} copy(bf16[4,768,256]{2,1,0:T(8,128)(2,1)S(1)} %fusion.15) | data formatting | bytes 3145728 | tf_op jit(solution)/shard_map/convert_element_type | solution.py:41
  50.7 10.9 %all-to-all-done = bf16[16,96,192]{2,0,1:T(8,128)(2,1)} async-done(((bf16[16,96,192]{2,0,1:T(8,128)(2,1)}), bf16[16,96,192]{2,0,1:T(8,128)(2,1)}, u32[]{:S(2)}, u32[]{:S(2)}) %all-to-all-start) | async-done | bytes 589856 | tf_op jit(solution)/shard_map/all_to_all | solution.py:38
  61.7 6.0 %all-to-all-start.2 = ((bf16[4,768,256]{2,0,1:T(4,128)(2,1)}), bf16[4,768,256]{2,0,1:T(4,128)(2,1)S(1)}, u32[]{:S(2)}, u32[]{:S(2)}) async-start(bf16[4,768,256]{2,0,1:T(4,128)(2,1)} %copy.20), calls=%async_computation.2 | async-start | bytes 3145728 | tf_op jit(solution)/shard_map/all_to_all | solution.py:42
  67.8 0.1 fusion.23
  67.9 1.2 copy.18
  69.1 0.1 fusion.16
  69.2 33.1 %all-to-all-done.2 = bf16[4,768,256]{2,0,1:T(4,128)(2,1)S(1)} async-done(((bf16[4,768,256]{2,0,1:T(4,128)(2,1)}), bf16[4,768,256]{2,0,1:T(4,128)(2,1)S(1)}, u32[]{:S(2)}, u32[]{:S(2)}) %all-to-all-start.2) | async-done | bytes 1572896 | tf_op jit(solution)/shard_map/all_to_all | solution.py:42
  102.3 0.9 copy_bitcast_fusion
  103.2 0.8 add_convert_fusion.1
  104.0 0.2 add.47
  104.2 0.2 sub.25
  104.4 0.0 copy-done
  104.4 4.4 %fusion.3 = bf16[2,12,192,2,256]{4,2,3,1,0:T(8,128)(2,1)} fusion(bf16[2,64,12,192,1]{3,1,0,2,4:T(8,128)(2,1)S(1)} %fusion.16, bf16[256,256]{1,0:T(8,128)(2,1)S(1)} %copy-done, bf16[1,64,2,12,256]{4,1,3,2,0:T(8,128)(2,1)S(1)} %sub.25, bf16[1,64,2,12,256]{4,1,3,2,0:T(8,128)(2,1)S(1)} %add.47), kind=kOutput, calls=%fused_computation.4 | convolution fusion | flops 1513095168 | bytes 7012352 | tf_op jit(solution)/shard_map/qmkpc,dc->qmkpd/dot_general | solution.py:59
  108.8 3.3 %convert_bitcast_fusion = f32[2,64,2,12,256]{4,1,2,3,0:T(8,128)S(1)} fusion(bf16[2,12,192,2,256]{4,2,3,1,0:T(8,128)(2,1)} %fusion.3, bf16[2,64,12,192,1]{3,1,0,2,4:T(8,128)(2,1)S(1)} %fusion.16), kind=kOutput, calls=%fused_computation.10 | convolution fusion | flops 303562752 | bytes 8454144 | tf_op jit(solution)/shard_map/qrmk,qmkpc->qrpmc/dot_general | solution.py:62
  112.1 0.5 add_convert_fusion
  112.6 0.1 pad_maximum_fusion.1
  112.8 0.1 copy.26
  112.9 0.9 copy.27
  113.8 42.6 %all_to_all.69 = bf16[128,24,256]{2,1,0:T(8,128)(2,1)S(1)} all-to-all(bf16[128,24,256]{2,1,0:T(8,128)(2,1)S(1)} %copy.27), channel_id=1, replica_groups=mesh['lat'=8,'lon'=4] {'lat','lon'}, dimensions={0} | all-to-all | bytes 3145728 | tf_op jit(solution)/shard_map/all_to_all | solution.py:67
  156.4 0.0 copy-start.4
  156.4 0.1 copy.28
  156.5 1.5 copy-done.4
  158.0 2.5 %fusion.7 = bf16[4,1440,256]{2,1,0:T(8,128)(2,1)S(1)} fusion(bf16[768,1440,1]{0,1,2:T(8,128)(2,1)S(1)} %copy-done.4, bf16[4,768,256]{2,1,0:T(8,128)(2,1)S(1)} %bitcast.64), kind=kOutput, calls=%fused_computation.8 | convolution fusion | flops 2266398720 | bytes 6733824 | tf_op jit(solution)/shard_map/kl,rkc->rlc/dot_general | solution.py:68
  160.5 15.0 %copy.29 = bf16[4,1440,256]{2,0,1:T(4,128)(2,1)S(1)} copy(bf16[4,1440,256]{2,1,0:T(8,128)(2,1)S(1)} %fusion.7) | data formatting | bytes 5898240 | tf_op jit(solution)/shard_map/convert_element_type | solution.py:70
  175.5 37.6 %all_to_all.70 = bf16[4,1440,256]{2,0,1:T(4,128)(2,1)S(1)} all-to-all(bf16[4,1440,256]{2,0,1:T(4,128)(2,1)S(1)} %copy.29), channel_id=1, replica_groups=mesh['lat'=8,'lon'=4] {'lon'}, dimensions={1} | all-to-all | bytes 5898240 | tf_op jit(solution)/shard_map/all_to_all | solution.py:71
  213.1 0.0 copy-start.1
  213.1 0.0 copy-start.2
  213.1 0.5 copy.30
  213.6 1.3 copy-done.1
  214.9 0.0 copy-done.2
  214.9 2.9 %fusion = bf16[16,360,256]{2,1,0:T(8,128)(2,1)} fusion(f32[4,4,360,256]{3,2,0,1:T(8,128)S(1)} %copy.30, bf16[16,360,256]{2,1,0:T(8,128)(2,1)S(1)} %copy-done.1, bf16[256,256]{1,0:T(8,128)(2,1)S(1)} %copy-done.2), kind=kOutput, calls=%fused_computation.1 | convolution fusion | flops 757923840 | bytes 11927552 | tf_op jit(solution)/shard_map/dot_general | solution.py:72
  (5 shorter events, 0.0 us)
Async XLA Ops:
  0.0 104.4 %copy-start = (bf16[256,256]{1,0:T(8,128)(2,1)S(1)}, bf16[256,256]{1,0:T(8,128)(2,1)}, u32[]{:S(2)}) copy-start(bf16[256,256]{1,0:T(8,128)(2,1)} %param.7) | copy-start | bytes 393220
  0.0 38.4 %all-to-all-start.1 = ((bf16[16,360,256]{2,1,0:T(8,128)(2,1)}), bf16[16,360,256]{2,1,0:T(8,128)(2,1)S(1)}, u32[]{:S(2)}, u32[]{:S(2)}) async-start(bf16[16,360,256]{2,1,0:T(8,128)(2,1)} %param.5), calls=%async_computation.1 | async-start | bytes 5898240 | tf_op jit(solution)/shard_map/all_to_all | solution.py:36
  38.4 23.2 %all-to-all-start = ((bf16[16,96,192]{2,0,1:T(8,128)(2,1)}), bf16[16,96,192]{2,0,1:T(8,128)(2,1)}, u32[]{:S(2)}, u32[]{:S(2)}) async-start(bf16[16,96,192]{2,0,1:T(8,128)(2,1)} %copy.17), calls=%async_computation | async-start | bytes 1572864 | tf_op jit(solution)/shard_map/all_to_all | solution.py:38
  44.1 1.6 copy-start.3
  61.7 40.7 %all-to-all-start.2 = ((bf16[4,768,256]{2,0,1:T(4,128)(2,1)}), bf16[4,768,256]{2,0,1:T(4,128)(2,1)S(1)}, u32[]{:S(2)}, u32[]{:S(2)}) async-start(bf16[4,768,256]{2,0,1:T(4,128)(2,1)} %copy.20), calls=%async_computation.2 | async-start | bytes 3145728 | tf_op jit(solution)/shard_map/all_to_all | solution.py:42
  156.4 1.6 copy-start.4
  213.1 1.8 copy-start.1
  213.1 1.8 copy-start.2

commit v2 on v1

--- a/solution.py
+++ b/solution.py
@@ -5,6 +5,8 @@
 import jax.numpy as jnp
 import numpy as np
 from jax import lax
+from jax.experimental import pallas as pl
+from jax.experimental.pallas import tpu as pltpu
 from jax.sharding import PartitionSpec as P
 
 BOTH = ("lat", "lon")
@@ -23,6 +25,75 @@
     return table.reshape(-1, count_lon).astype(jnp.bfloat16)
 
 
+def exchange_kernel(
+    lat_count, lon_count, cot_ref, leg_ref, rows_ref, basis_ref,
+    cot_send, cot_recv, leg_send, leg_recv, own_sem,
+):
+    lat, lon = lax.axis_index("lat"), lax.axis_index("lon")
+    barrier = pltpu.get_barrier_semaphore()
+    partners = [(lat, lax.rem(lon + step, lon_count)) for step in range(1, lon_count)]
+    partners += [(lax.rem(lat + step, lat_count), lon) for step in range(1, lat_count)]
+    for partner in partners:
+        pl.semaphore_signal(
+            barrier, inc=1, device_id=partner, device_id_type=pl.DeviceIdType.MESH
+        )
+    pl.semaphore_wait(barrier, len(partners))
+    copies = []
+    for step in range(1, lon_count):
+        there = lax.rem(lon + step, lon_count)
+        copies.append(
+            pltpu.make_async_remote_copy(
+                src_ref=cot_ref.at[there],
+                dst_ref=rows_ref.at[:, lon],
+                send_sem=cot_send.at[step],
+                recv_sem=cot_recv.at[step],
+                device_id=(lat, there),
+                device_id_type=pl.DeviceIdType.MESH,
+            )
+        )
+    for step in range(1, lat_count):
+        there = lax.rem(lat + step, lat_count)
+        copies.append(
+            pltpu.make_async_remote_copy(
+                src_ref=leg_ref.at[there],
+                dst_ref=basis_ref.at[lat],
+                send_sem=leg_send.at[step],
+                recv_sem=leg_recv.at[step],
+                device_id=(there, lon),
+                device_id_type=pl.DeviceIdType.MESH,
+            )
+        )
+    copies.append(pltpu.make_async_copy(cot_ref.at[lon], rows_ref.at[:, lon], own_sem.at[0]))
+    copies.append(pltpu.make_async_copy(leg_ref.at[lat], basis_ref.at[lat], own_sem.at[1]))
+    for copy in copies:
+        copy.start()
+    for copy in copies:
+        copy.wait()
+
+
+def exchange(cotangent, basis, lat_count, lon_count):
+    lat_rows, lon_dev, width = cotangent.shape
+    rows_each = lat_rows // lon_count
+    anywhere = pl.BlockSpec(memory_space=pl.ANY)
+    return pl.pallas_call(
+        functools.partial(exchange_kernel, lat_count, lon_count),
+        out_shape=(
+            jax.ShapeDtypeStruct((rows_each, lon_count, lon_dev, width), jnp.bfloat16),
+            jax.ShapeDtypeStruct(basis.shape, jnp.bfloat16),
+        ),
+        in_specs=[anywhere] * 2,
+        out_specs=(anywhere, anywhere),
+        scratch_shapes=[
+            pltpu.SemaphoreType.DMA((lon_count,)),
+            pltpu.SemaphoreType.DMA((lon_count,)),
+            pltpu.SemaphoreType.DMA((lat_count,)),
+            pltpu.SemaphoreType.DMA((lat_count,)),
+            pltpu.SemaphoreType.DMA((2,)),
+        ],
+        compiler_params=pltpu.CompilerParams(collective_id=0, has_side_effects=True),
+    )(cotangent.reshape(lon_count, rows_each, lon_dev, width), basis)
+
+
 def shards(table, cotangent, legendre, spectral_weight, skip_weight):
     lat_rows, lon_dev, width = cotangent.shape
     lat_count = lax.axis_size("lat")
@@ -33,9 +104,10 @@
     half_rows = count_lat // 2
     fourier = jnp.asarray(table)
 
-    rows = lax.all_to_all(cotangent, "lon", split_axis=0, concat_axis=1, tiled=True)
     padded = jnp.pad(legendre, ((0, 0), (0, wave_each * lat_count - wave_dev), (0, 0)))
-    basis = lax.all_to_all(padded, "lat", split_axis=1, concat_axis=0, tiled=True)
+    padded = padded.reshape(lat_rows, lat_count, wave_each, half_deg).transpose(1, 2, 0, 3)
+    rows, basis = exchange(cotangent, padded, lat_count, lon_count)
+    rows = rows.reshape(-1, lon_dev * lon_count, width)
     spectra = jnp.einsum(
         "kl,rlc->rkc", fourier, rows, preferred_element_type=jnp.float32
     ).astype(jnp.bfloat16)
@@ -43,24 +115,26 @@
     coeffs = coeffs.reshape(2, half_rows, 2, wave_each, width)
 
     wave_start = lax.axis_index("lon") * wave_dev + lax.axis_index("lat") * wave_each
-    wavenum = wave_start + lax.broadcasted_iota(jnp.int32, (2, 1, wave_each, half_deg), 2)
-    degree = 2 * lax.broadcasted_iota(jnp.int32, (2, 1, wave_each, half_deg), 3)
-    half = lax.broadcasted_iota(jnp.int32, (2, 1, wave_each, half_deg), 0)
+    extent = (2, 1, wave_each, 1, half_deg)
+    wavenum = wave_start + lax.broadcasted_iota(jnp.int32, extent, 2)
+    degree = 2 * lax.broadcasted_iota(jnp.int32, extent, 4)
+    half = lax.broadcasted_iota(jnp.int32, extent, 0)
     parity = wavenum % 2
     degree = degree + jnp.where(half == 0, parity, 1 - parity)
-    basis = basis.reshape(2, half_rows, wave_each, half_deg)
+    basis = basis.reshape(2, lat_count // 2, wave_each, lat_rows, half_deg)
     basis = jnp.where(degree >= wavenum, basis, jnp.zeros_like(basis))
+    basis = basis.transpose(0, 2, 1, 3, 4).reshape(2, wave_each, half_rows, half_deg)
 
     wide = coeffs.astype(jnp.float32)
     combined = jnp.stack([wide[0] + wide[1], wide[0] - wide[1]]).astype(jnp.bfloat16)
     sums = jnp.einsum(
-        "qrmk,qrpmc->qmkpc", basis, combined, preferred_element_type=jnp.float32
+        "qmrk,qrpmc->qmkpc", basis, combined, preferred_element_type=jnp.float32
     ).astype(jnp.bfloat16)
     mixed = jnp.einsum(
         "qmkpc,dc->qmkpd", sums, spectral_weight, preferred_element_type=jnp.float32
     ).astype(jnp.bfloat16)
     projected = jnp.einsum(
-        "qrmk,qmkpc->qrpmc", basis, mixed, preferred_element_type=jnp.float32
+        "qmrk,qmkpc->qrpmc", basis, mixed, preferred_element_type=jnp.float32
     ).astype(jnp.bfloat16).astype(jnp.float32)
     grads = jnp.stack([projected[0] + projected[1], projected[0] - projected[1]])
     grads = grads.astype(jnp.bfloat16).reshape(count_lat, 2 * wave_each, width)
@@ -68,7 +142,9 @@
     grid_part = jnp.einsum(
         "kl,rkc->rlc", fourier, grads, preferred_element_type=jnp.float32
     ).astype(jnp.bfloat16)
-    spatial = lax.all_to_all(grid_part, "lon", split_axis=1, concat_axis=0, tiled=True)
+    grid_part = grid_part.reshape(-1, lon_count, lon_dev, width).transpose(1, 0, 2, 3)
+    spatial = lax.all_to_all(grid_part, "lon", split_axis=0, concat_axis=0, tiled=True)
+    spatial = spatial.reshape(cotangent.shape)
     skip_term = jnp.dot(
         cotangent.reshape(-1, width), skip_weight.T, preferred_element_type=jnp.float32
     ).reshape(cotangent.shape)

time: 221 us -> 189 us (0.86)
  waiting for transfers between devices: 75.5 us -> 34.2 us
  Pallas kernels: 0 us -> 36.7 us
  local copies, waits for them, and re-layouts: 27.5 us -> 10.6 us
  starting transfers between devices: 16.2 us -> 4.28 us
    all_to_all x2 -> x0, waiting for transfers between devices: 42.4 us -> none  [the longest x1 31.5 us: shards(): lax.all_to_all(cotangent, 'lon', split_axis=0, concat_axis=1, tiled=True)]
    pallas_call x0 -> x1, Pallas kernels: none -> 36.7 us  [exchange(): pl.pallas_call(functools.partial(exchange_kernel, lat_count, lon_count),...]
    convert_element_type x2 -> x0, local copies, waits for them, and re-layouts: 15.5 us -> none  [the longest x1 15 us: shards(): grid_part = jnp.einsum('kl,rkc->rlc', fourier, grads, preferred_element_t...]
    all_to_all x2 -> x0, starting transfers between devices: 10.1 us -> none  [the longest x1 5.66 us: shards(): lax.all_to_all(padded, 'lat', split_axis=1, concat_axis=0, tiled=True)]
    dot_general x1, matrix products: 2.64 us -> 5.19 us  [shards(): jnp.einsum('kl,rlc->rkc', fourier, rows, preferred_element_type=jnp.float32)]
    unnamed x11 -> x13, local copies, waits for them, and re-layouts: 6.74 us -> 4.34 us
  transfers between devices with their start and end apart: 3 -> 1, of which waited for: 3 -> 1; matrix products, arithmetic and copies ran while one was open for 4% -> 0% of each run, Pallas kernels for 0% -> 0%
where the time goes in v2:
time: 189 us; the launch traced here: 186 us
  blocking collectives  80.5 us (43%)
  Pallas kernels  36.7 us (19%)
  waiting for transfers between devices  34.2 us (18%)
  matrix products  18 us (10%)
  local copies, waits for them, and re-layouts  10.6 us (6%)
  starting transfers between devices  4.28 us (2%)
    all_to_all x1, blocking collectives, shards(): grads = lax.all_to_all(grads, BOTH, split_axis=0, concat_axis=1, tiled=True)  42.6 us
    all_to_all x1, blocking collectives, shards(): lax.all_to_all(grid_part, 'lon', split_axis=0, concat_axis=0, tiled=True)  37.8 us
    pallas_call x1, Pallas kernels, exchange(): pl.pallas_call(functools.partial(exchange_kernel, lat_count, lon_count),...  36.7 us
    all_to_all x1, waiting for transfers between devices, shards(): lax.all_to_all(spectra, BOTH, split_axis=1, concat_axis=0, tiled=True)  34.2 us
    dot_general x1, matrix products, shards(): jnp.einsum('kl,rlc->rkc', fourier, rows, preferred_element_type=jnp.float32)  5.19 us
    dot_general x1, matrix products, shards(): jnp.einsum('qmkpc,dc->qmkpd', sums, spectral_weight, preferred_element_ty...  4.4 us
    unnamed x13, local copies, waits for them, and re-layouts  4.34 us
    all_to_all x1, starting transfers between devices, shards(): lax.all_to_all(spectra, BOTH, split_axis=1, concat_axis=0, tiled=True)  4.28 us
  transfers between devices with their start and end apart: 1, of which 1 were waited for; matrix products, arithmetic and copies ran while one was open for 0% of the time, Pallas kernels for 0%

profile of v2, /device:TPU:11, one launch (start us, length us, event | category | flops | bytes accessed | tf_op | source)
XLA Modules:
  0.0 185.9 jit_solution(9053444532484045514)
XLA Ops:
  0.0 0.0 copy-start
  0.0 2.5 %copy.18 = bf16[16,96,192]{2,0,1:T(8,128)(2,1)} copy(bf16[16,96,192]{2,1,0:T(8,128)(2,1)} %param.6) | data formatting | bytes 1179648 | tf_op args[1]
  2.5 36.7 %shard_map.55 = (bf16[4,4,360,256]{3,2,1,0:T(8,128)(2,1)}, bf16[8,12,16,192]{3,2,1,0:T(8,128)(2,1)}) custom-call(bf16[4,4,360,256]{3,2,1,0:T(8,128)(2,1)} %bitcast.56, bf16[8,12,16,192]{3,2,1,0:T(8,128)(2,1)} %bitcast.63), custom_call_target="tpu_custom_call" | custom-call | tf_op jit(solution)/shard_map/pallas_call | solution.py:78
  39.2 5.2 %fusion.14 = bf16[4,768,256]{1,2,0:T(8,128)(2,1)S(1)} fusion(bf16[4,1440,256]{2,1,0:T(8,128)(2,1)} %bitcast.67, bf16[768,1440,1]{0,1,2:T(8,128)(2,1)} %constant.37), kind=kOutput, calls=%fused_computation.20 | convolution fusion | flops 2265710592 | bytes 6733824 | tf_op jit(solution)/shard_map/kl,rlc->rkc/dot_general | solution.py:111
  44.4 2.2 %copy.20 = bf16[4,768,256]{2,0,1:T(4,128)(2,1)} copy(bf16[4,768,256]{1,2,0:T(8,128)(2,1)S(1)} %fusion.14) | data formatting | bytes 3145728 | tf_op jit(solution)/shard_map/convert_element_type | solution.py:113
  46.6 0.0 copy-start.2
  46.6 4.3 %all-to-all-start = ((bf16[4,768,256]{2,0,1:T(4,128)(2,1)}), bf16[4,768,256]{2,0,1:T(4,128)(2,1)S(1)}, u32[]{:S(2)}, u32[]{:S(2)}) async-start(bf16[4,768,256]{2,0,1:T(4,128)(2,1)} %copy.20), calls=%async_computation | async-start | bytes 3145728 | tf_op jit(solution)/shard_map/all_to_all | solution.py:114
  50.9 0.1 fusion.18
  51.0 0.0 copy-done.2
  51.0 0.1 select_bitcast_fusion
  51.1 0.1 copy.19
  51.2 34.2 %all-to-all-done = bf16[4,768,256]{2,0,1:T(4,128)(2,1)S(1)} async-done(((bf16[4,768,256]{2,0,1:T(4,128)(2,1)}), bf16[4,768,256]{2,0,1:T(4,128)(2,1)S(1)}, u32[]{:S(2)}, u32[]{:S(2)}) %all-to-all-start) | async-done | bytes 1572896 | tf_op jit(solution)/shard_map/all_to_all | solution.py:114
  85.4 0.2 copy.21
  85.6 0.3 convert_bitcast_fusion
  85.9 0.4 add_convert_fusion.1
  86.3 0.6 copy.22
  86.9 1.1 add.47
  88.0 0.0 copy-start.3
  88.0 0.6 copy.23
  88.6 0.2 sub.25
  88.8 0.0 copy-done
  88.8 0.3 copy-done.3
  89.1 4.4 %fusion.3 = bf16[2,12,192,2,256]{4,2,3,1,0:T(8,128)(2,1)} fusion(bf16[2,12,64,192,1]{3,2,4,1,0:T(8,128)(2,1)S(1)} %bitcast.61, bf16[256,256]{1,0:T(8,128)(2,1)S(1)} %copy-done, bf16[1,64,2,12,256]{4,1,3,2,0:T(8,128)(2,1)S(1)} %sub.25, bf16[1,64,2,12,256]{4,1,3,2,0:T(8,128)(2,1)S(1)} %copy-done.3), kind=kOutput, calls=%fused_computation.4 | convolution fusion | flops 1513095168 | bytes 7012352 | tf_op jit(solution)/shard_map/qmkpc,dc->qmkpd/dot_general | solution.py:133
  93.5 3.3 %convert_bitcast_fusion.1 = f32[2,64,2,12,256]{4,1,2,3,0:T(8,128)S(1)} fusion(bf16[2,12,64,192,1]{3,2,4,1,0:T(8,128)(2,1)S(1)} %bitcast.62, bf16[2,12,192,2,256]{4,2,3,1,0:T(8,128)(2,1)} %fusion.3), kind=kOutput, calls=%fused_computation.9 | convolution fusion | flops 303562752 | bytes 8454144 | tf_op jit(solution)/shard_map/qmrk,qmkpc->qrpmc/dot_general | solution.py:136
  96.9 0.5 add_convert_fusion
  97.4 0.1 pad_maximum_fusion.1
  97.5 0.1 copy.26
  97.6 0.9 copy.27
  98.5 42.6 %all_to_all.32 = bf16[128,24,256]{2,1,0:T(8,128)(2,1)S(1)} all-to-all(bf16[128,24,256]{2,1,0:T(8,128)(2,1)S(1)} %copy.27), channel_id=1, replica_groups=mesh['lat'=8,'lon'=4] {'lat','lon'}, dimensions={0} | all-to-all | bytes 3145728 | tf_op jit(solution)/shard_map/all_to_all | solution.py:141
  141.2 0.0 copy-start.5
  141.2 0.1 copy.28
  141.3 1.5 copy-done.5
  142.8 2.5 %convolution_convert_fusion = bf16[4,256,1440]{1,2,0:T(8,128)(2,1)S(1)} fusion(bf16[768,1440,1]{0,1,2:T(8,128)(2,1)S(1)} %copy-done.5, bf16[4,768,256]{2,1,0:T(8,128)(2,1)S(1)} %bitcast.65), kind=kOutput, calls=%fused_computation.7 | convolution fusion | flops 2266398720 | bytes 6733824 | tf_op jit(solution)/shard_map/kl,rkc->rlc/dot_general | solution.py:142
  145.3 0.2 copy.37
  145.5 0.0 copy-start.1
  145.5 0.0 copy-start.4
  145.5 37.8 %all_to_all.33 = bf16[4,4,360,256]{3,2,1,0:T(8,128)(2,1)S(1)} all-to-all(bf16[4,4,360,256]{3,2,1,0:T(8,128)(2,1)S(1)} %bitcast.57), channel_id=1, replica_groups=mesh['lat'=8,'lon'=4] {'lon'}, dimensions={0} | all-to-all | bytes 5898240 | tf_op jit(solution)/shard_map/all_to_all | solution.py:146
  183.3 0.0 copy-done.1
  183.3 0.0 copy-done.4
  183.3 2.6 %fusion = bf16[16,360,256]{2,1,0:T(8,128)(2,1)} fusion(bf16[4,4,360,256]{3,2,1,0:T(8,128)(2,1)S(1)} %all_to_all.33, bf16[16,360,256]{2,1,0:T(8,128)(2,1)S(1)} %copy-done.1, bf16[256,256]{1,0:T(8,128)(2,1)S(1)} %copy-done.4), kind=kOutput, calls=%fused_computation.1 | convolution fusion | flops 759398400 | bytes 8978432 | tf_op jit(solution)/shard_map/dot_general | solution.py:148
  (5 shorter events, 0.0 us)
Async XLA Ops:
  0.0 88.8 %copy-start = (bf16[256,256]{1,0:T(8,128)(2,1)S(1)}, bf16[256,256]{1,0:T(8,128)(2,1)}, u32[]{:S(2)}) copy-start(bf16[256,256]{1,0:T(8,128)(2,1)} %param.7) | copy-start | bytes 393220
  46.6 4.5 %copy-start.2 = (bf16[8,12,16,192]{3,2,1,0:T(8,128)(2,1)S(1)}, bf16[8,12,16,192]{3,2,1,0:T(8,128)(2,1)}, u32[]{:S(2)}) copy-start(bf16[8,12,16,192]{3,2,1,0:T(8,128)(2,1)} %get-tuple-element.7) | copy-start | bytes 1769476
  46.6 38.8 %all-to-all-start = ((bf16[4,768,256]{2,0,1:T(4,128)(2,1)}), bf16[4,768,256]{2,0,1:T(4,128)(2,1)S(1)}, u32[]{:S(2)}, u32[]{:S(2)}) async-start(bf16[4,768,256]{2,0,1:T(4,128)(2,1)} %copy.20), calls=%async_computation | async-start | bytes 3145728 | tf_op jit(solution)/shard_map/all_to_all | solution.py:114
  88.0 1.1 copy-start.3
  141.2 1.6 copy-start.5
  145.5 37.9 %copy-start.1 = (bf16[16,360,256]{2,1,0:T(8,128)(2,1)S(1)}, bf16[16,360,256]{2,1,0:T(8,128)(2,1)}, u32[]{:S(2)}) copy-start(bf16[16,360,256]{2,1,0:T(8,128)(2,1)} %param.5) | copy-start | bytes 8847364
  145.5 37.9 %copy-start.4 = (bf16[256,256]{1,0:T(8,128)(2,1)S(1)}, bf16[256,256]{1,0:T(8,128)(2,1)}, u32[]{:S(2)}) copy-start(bf16[256,256]{1,0:T(8,128)(2,1)} %param.8) | copy-start | bytes 393220

commit v3 on v2

--- a/solution.py
+++ b/solution.py
@@ -94,6 +94,280 @@
     )(cotangent.reshape(lon_count, rows_each, lon_dev, width), basis)
 
 
+MESH = pl.DeviceIdType.MESH
+
+
+def place_of(index, lon_count):
+    return (lax.div(index, lon_count), lax.rem(index, lon_count))
+
+
+def greet_all(total, me, lon_count):
+    barrier = pltpu.get_barrier_semaphore()
+
+    def greet(step, carry):
+        there = place_of(lax.rem(me + step, total), lon_count)
+        pl.semaphore_signal(barrier, inc=1, device_id=there, device_id_type=MESH)
+        return carry
+
+    lax.fori_loop(1, total, greet, 0)
+    pl.semaphore_wait(barrier, total - 1)
+
+
+def forward_kernel(
+    lat_count, lon_count, cot_ref, leg_ref, table_ref, coeffs_ref, basis_ref,
+    rows, spectra, cot_send, cot_recv, leg_send, leg_recv, all_send, all_recv, own_cot, own_leg,
+    own_all,
+):
+    lat, lon = lax.axis_index("lat"), lax.axis_index("lon")
+    total = lat_count * lon_count
+    me = lat * lon_count + lon
+    row_count = rows.shape[0]
+    greet_all(total, me, lon_count)
+
+    def row_copies(row):
+        copies = []
+        for step in range(1, lon_count):
+            there = lax.rem(lon + step, lon_count)
+            copies.append(
+                pltpu.make_async_remote_copy(
+                    src_ref=cot_ref.at[there, row],
+                    dst_ref=rows.at[row, lon],
+                    send_sem=cot_send.at[row, step],
+                    recv_sem=cot_recv.at[row, step],
+                    device_id=(lat, there),
+                    device_id_type=MESH,
+                )
+            )
+        copies.append(
+            pltpu.make_async_copy(cot_ref.at[lon, row], rows.at[row, lon], own_cot.at[row])
+        )
+        return copies
+
+    def start_row(row):
+        for copy in row_copies(row):
+            copy.start()
+
+    leg_copies = []
+    for step in range(1, lat_count):
+        there = lax.rem(lat + step, lat_count)
+        leg_copies.append(
+            pltpu.make_async_remote_copy(
+                src_ref=leg_ref.at[there],
+                dst_ref=basis_ref.at[lat],
+                send_sem=leg_send.at[step],
+                recv_sem=leg_recv.at[step],
+                device_id=(there, lon),
+                device_id_type=MESH,
+            )
+        )
+    leg_copies.append(pltpu.make_async_copy(leg_ref.at[lat], basis_ref.at[lat], own_leg))
+
+    def all_copy(row, step):
+        there = lax.rem(me + step, total)
+        return pltpu.make_async_remote_copy(
+            src_ref=spectra.at[row, there],
+            dst_ref=coeffs_ref.at[me, row],
+            send_sem=all_send.at[row, step],
+            recv_sem=all_recv.at[row, step],
+            device_id=place_of(there, lon_count),
+            device_id_type=MESH,
+        )
+
+    def own_copy(row):
+        return pltpu.make_async_copy(spectra.at[row, me], coeffs_ref.at[me, row], own_all.at[row])
+
+    for row in range(min(2, row_count)):
+        start_row(row)
+    for copy in leg_copies:
+        copy.start()
+
+    def transform(row, carry):
+        for copy in row_copies(row):
+            copy.wait()
+
+        @pl.when(row + 2 < row_count)
+        def _():
+            start_row(row + 2)
+
+        value = jnp.dot(table_ref[0], rows[row, 0], preferred_element_type=jnp.float32)
+        for block in range(1, lon_count):
+            value += jnp.dot(
+                table_ref[block], rows[row, block], preferred_element_type=jnp.float32
+            )
+        spectra[row] = value.reshape(spectra.shape[1:]).astype(jnp.bfloat16)
+
+        def send(step, inner):
+            all_copy(row, step).start()
+            return inner
+
+        lax.fori_loop(1, total, send, 0)
+        own_copy(row).start()
+        return carry
+
+    lax.fori_loop(0, row_count, transform, 0)
+
+    def finish(row, carry):
+        def arrived(step, inner):
+            all_copy(row, step).wait()
+            return inner
+
+        lax.fori_loop(1, total, arrived, 0)
+        own_copy(row).wait()
+        return carry
+
+    lax.fori_loop(0, row_count, finish, 0)
+    for copy in leg_copies:
+        copy.wait()
+
+
+def backward_kernel(
+    lat_count, lon_count, grads_ref, table_ref, spatial_ref,
+    held, stage, all_send, all_recv, lon_send, lon_recv, own_all, own_lon,
+):
+    lat, lon = lax.axis_index("lat"), lax.axis_index("lon")
+    total = lat_count * lon_count
+    me = lat * lon_count + lon
+    row_count = held.shape[0]
+    greet_all(total, me, lon_count)
+
+    def all_copy(row, step):
+        there = lax.rem(me + step, total)
+        return pltpu.make_async_remote_copy(
+            src_ref=grads_ref.at[there, row],
+            dst_ref=held.at[row, me],
+            send_sem=all_send.at[row, step],
+            recv_sem=all_recv.at[row, step],
+            device_id=place_of(there, lon_count),
+            device_id_type=MESH,
+        )
+
+    def own_copy(row):
+        return pltpu.make_async_copy(grads_ref.at[me, row], held.at[row, me], own_all.at[row])
+
+    def start_row(row):
+        def send(step, inner):
+            all_copy(row, step).start()
+            return inner
+
+        lax.fori_loop(1, total, send, 0)
+        own_copy(row).start()
+
+    def wait_row(row):
+        def arrived(step, inner):
+            all_copy(row, step).wait()
+            return inner
+
+        lax.fori_loop(1, total, arrived, 0)
+        own_copy(row).wait()
+
+    def row_copies(row):
+        copies = []
+        for step in range(1, lon_count):
+            there = lax.rem(lon + step, lon_count)
+            copies.append(
+                pltpu.make_async_remote_copy(
+                    src_ref=stage.at[row, there],
+                    dst_ref=spatial_ref.at[lon, row],
+                    send_sem=lon_send.at[row, step],
+                    recv_sem=lon_recv.at[row, step],
+                    device_id=(lat, there),
+                    device_id_type=MESH,
+                )
+            )
+        copies.append(
+            pltpu.make_async_copy(stage.at[row, lon], spatial_ref.at[lon, row], own_lon.at[row])
+        )
+        return copies
+
+    for row in range(min(2, row_count)):
+        start_row(row)
+
+    def transform(row, carry):
+        wait_row(row)
+
+        @pl.when(row + 2 < row_count)
+        def _():
+            start_row(row + 2)
+
+        depth = held.shape[1] * held.shape[2]
+        value = held[row].astype(jnp.float32).reshape(depth, -1).astype(jnp.bfloat16)
+        for block in range(lon_count):
+            stage[row, block] = jnp.dot(
+                table_ref[block], value, preferred_element_type=jnp.float32
+            ).astype(jnp.bfloat16)
+        for copy in row_copies(row):
+            copy.start()
+        return carry
+
+    lax.fori_loop(0, row_count, transform, 0)
+
+    def finish(row, carry):
+        for copy in row_copies(row):
+            copy.wait()
+        return carry
+
+    lax.fori_loop(0, row_count, finish, 0)
+
+
+def forward(cotangent, basis, table, lat_count, lon_count, waves):
+    lat_rows, lon_dev, width = cotangent.shape
+    rows_each, total = lat_rows // lon_count, lat_count * lon_count
+    anywhere = pl.BlockSpec(memory_space=pl.ANY)
+    dma = pltpu.SemaphoreType.DMA
+    blocks = table.reshape(-1, lon_count, lon_dev).transpose(1, 0, 2)
+    return pl.pallas_call(
+        functools.partial(forward_kernel, lat_count, lon_count),
+        out_shape=(
+            jax.ShapeDtypeStruct((total, rows_each, waves, width), jnp.bfloat16),
+            jax.ShapeDtypeStruct(basis.shape, jnp.bfloat16),
+        ),
+        in_specs=[anywhere, anywhere, pl.BlockSpec(memory_space=pltpu.VMEM)],
+        out_specs=(anywhere, anywhere),
+        scratch_shapes=[
+            pltpu.VMEM((rows_each, lon_count, lon_dev, width), jnp.bfloat16),
+            pltpu.VMEM((rows_each, total, waves, width), jnp.bfloat16),
+            dma((rows_each, lon_count)),
+            dma((rows_each, lon_count)),
+            dma((lat_count,)),
+            dma((lat_count,)),
+            dma((rows_each, total)),
+            dma((rows_each, total)),
+            dma((rows_each,)),
+            dma,
+            dma((rows_each,)),
+        ],
+        compiler_params=pltpu.CompilerParams(
+            collective_id=1, has_side_effects=True, vmem_limit_bytes=40 * 2**20
+        ),
+    )(cotangent.reshape(lon_count, rows_each, lon_dev, width), basis, jnp.asarray(blocks))
+
+
+def backward(grads, table, lat_count, lon_count, lon_dev):
+    total, rows_each, waves, width = grads.shape
+    anywhere = pl.BlockSpec(memory_space=pl.ANY)
+    dma = pltpu.SemaphoreType.DMA
+    blocks = table.reshape(-1, lon_count, lon_dev).transpose(1, 2, 0)
+    return pl.pallas_call(
+        functools.partial(backward_kernel, lat_count, lon_count),
+        out_shape=jax.ShapeDtypeStruct((lon_count, rows_each, lon_dev, width), jnp.bfloat16),
+        in_specs=[anywhere, pl.BlockSpec(memory_space=pltpu.VMEM)],
+        out_specs=anywhere,
+        scratch_shapes=[
+            pltpu.VMEM((rows_each, total, waves, width), jnp.bfloat16),
+            pltpu.VMEM((rows_each, lon_count, lon_dev, width), jnp.bfloat16),
+            dma((rows_each, total)),
+            dma((rows_each, total)),
+            dma((rows_each, lon_count)),
+            dma((rows_each, lon_count)),
+            dma((rows_each,)),
+            dma((rows_each,)),
+        ],
+        compiler_params=pltpu.CompilerParams(
+            collective_id=2, has_side_effects=True, vmem_limit_bytes=40 * 2**20
+        ),
+    )(grads, jnp.asarray(blocks))
+
+
 def shards(table, cotangent, legendre, spectral_weight, skip_weight):
     lat_rows, lon_dev, width = cotangent.shape
     lat_count = lax.axis_size("lat")
@@ -106,12 +380,17 @@
 
     padded = jnp.pad(legendre, ((0, 0), (0, wave_each * lat_count - wave_dev), (0, 0)))
     padded = padded.reshape(lat_rows, lat_count, wave_each, half_deg).transpose(1, 2, 0, 3)
-    rows, basis = exchange(cotangent, padded, lat_count, lon_count)
-    rows = rows.reshape(-1, lon_dev * lon_count, width)
-    spectra = jnp.einsum(
-        "kl,rlc->rkc", fourier, rows, preferred_element_type=jnp.float32
-    ).astype(jnp.bfloat16)
-    coeffs = lax.all_to_all(spectra, BOTH, split_axis=1, concat_axis=0, tiled=True)
+    waves = 2 * wave_each
+    fused = waves % 8 == 0 and lon_dev % 8 == 0
+    if fused:
+        coeffs, basis = forward(cotangent, padded, table, lat_count, lon_count, waves)
+    else:
+        rows, basis = exchange(cotangent, padded, lat_count, lon_count)
+        rows = rows.reshape(-1, lon_dev * lon_count, width)
+        spectra = jnp.einsum(
+            "kl,rlc->rkc", fourier, rows, preferred_element_type=jnp.float32
+        ).astype(jnp.bfloat16)
+        coeffs = lax.all_to_all(spectra, BOTH, split_axis=1, concat_axis=0, tiled=True)
     coeffs = coeffs.reshape(2, half_rows, 2, wave_each, width)
 
     wave_start = lax.axis_index("lon") * wave_dev + lax.axis_index("lat") * wave_each
@@ -138,12 +417,16 @@
     ).astype(jnp.bfloat16).astype(jnp.float32)
     grads = jnp.stack([projected[0] + projected[1], projected[0] - projected[1]])
     grads = grads.astype(jnp.bfloat16).reshape(count_lat, 2 * wave_each, width)
-    grads = lax.all_to_all(grads, BOTH, split_axis=0, concat_axis=1, tiled=True)
-    grid_part = jnp.einsum(
-        "kl,rkc->rlc", fourier, grads, preferred_element_type=jnp.float32
-    ).astype(jnp.bfloat16)
-    grid_part = grid_part.reshape(-1, lon_count, lon_dev, width).transpose(1, 0, 2, 3)
-    spatial = lax.all_to_all(grid_part, "lon", split_axis=0, concat_axis=0, tiled=True)
+    if fused:
+        grads = grads.reshape(lat_count * lon_count, -1, waves, width)
+        spatial = backward(grads, table, lat_count, lon_count, lon_dev)
+    else:
+        grads = lax.all_to_all(grads, BOTH, split_axis=0, concat_axis=1, tiled=True)
+        grid_part = jnp.einsum(
+            "kl,rkc->rlc", fourier, grads, preferred_element_type=jnp.float32
+        ).astype(jnp.bfloat16)
+        grid_part = grid_part.reshape(-1, lon_count, lon_dev, width).transpose(1, 0, 2, 3)
+        spatial = lax.all_to_all(grid_part, "lon", split_axis=0, concat_axis=0, tiled=True)
     spatial = spatial.reshape(cotangent.shape)
     skip_term = jnp.dot(
         cotangent.reshape(-1, width), skip_weight.T, preferred_element_type=jnp.float32

time: 189 us -> 166 us (0.88); the launches traced: 186 us -> 165 us
  Pallas kernels: 36.7 us -> 127 us
  blocking collectives: 80.5 us -> 0 us
  waiting for transfers between devices: 34.2 us -> 0 us
  local copies, waits for them, and re-layouts: 10.6 us -> 22.3 us
  matrix products: 18 us -> 12.7 us
  starting transfers between devices: 4.28 us -> 0 us
  other arithmetic: 1.51 us -> 3.42 us
    pallas_call x1 -> x2, Pallas kernels: 36.7 us -> 127 us  [the longest x1 64.3 us: backward(): pl.pallas_call(functools.partial(backward_kernel, lat_count, lon_count),...]
    all_to_all x2 -> x0, blocking collectives: 80.5 us -> none  [the longest x1 42.6 us: shards(): grads = lax.all_to_all(grads, BOTH, split_axis=0, concat_axis=1, tiled=True)]
    all_to_all x1 -> x0, waiting for transfers between devices: 34.2 us -> none  [shards(): lax.all_to_all(spectra, BOTH, split_axis=1, concat_axis=0, tiled=True)]
    unnamed x13 -> x14, local copies, waits for them, and re-layouts: 4.34 us -> 16.1 us
    dot_general x3 -> x1, matrix products: 12.1 us -> 3.61 us  [shards(): jnp.einsum('qmrk,qrpmc->qmkpc', basis, combined, preferred_element_type=j...]
    all_to_all x1 -> x0, starting transfers between devices: 4.28 us -> none  [shards(): lax.all_to_all(spectra, BOTH, split_axis=1, concat_axis=0, tiled=True)]
    convert_element_type x1 -> x2, local copies, waits for them, and re-layouts: 0.89 us -> 4.94 us  [shards(): grads = grads.astype(jnp.bfloat16).reshape(count_lat, 2 * wave_each, width)]
    dot_general x1, matrix products: 3.32 us -> 6.52 us  [shards(): jnp.einsum('qmrk,qmkpc->qrpmc', basis, mixed, preferred_element_type=jnp....]
  transfers between devices with their start and end apart: 1 -> 0, of which waited for: 1 -> 0; matrix products, arithmetic and copies ran while one was open for 0% -> 0% of each run, Pallas kernels for 0% -> 0%
where the time goes in v3:
time: 166 us; the launch traced here: 165 us
  Pallas kernels  127 us (77%)
  local copies, waits for them, and re-layouts  22.3 us (13%)
  matrix products  12.7 us (8%)
  other arithmetic  3.42 us (2%)
    pallas_call x1, Pallas kernels, backward(): pl.pallas_call(functools.partial(backward_kernel, lat_count, lon_count),...  64.3 us
    pallas_call x1, Pallas kernels, forward(): pl.pallas_call(functools.partial(forward_kernel, lat_count, lon_count), o...  62.3 us
    unnamed x14, local copies, waits for them, and re-layouts  16.1 us
    dot_general x1, matrix products, shards(): jnp.einsum('qmrk,qmkpc->qrpmc', basis, mixed, preferred_element_type=jnp....  6.52 us
    convert_element_type x2, local copies, waits for them, and re-layouts, shards(): grads = grads.astype(jnp.bfloat16).reshape(count_lat, 2 * wave_each, width)  4.94 us
    dot_general x1, matrix products, shards(): jnp.einsum('qmrk,qrpmc->qmkpc', basis, combined, preferred_element_type=j...  3.61 us

profile of v3, /device:TPU:11, one launch (start us, length us, event | category | flops | bytes accessed | tf_op | source)
XLA Modules:
  0.0 165.3 jit_solution(6353906458885919662)
XLA Ops:
  0.0 0.0 copy-start
  0.1 0.1 fusion.23
  0.2 1.6 copy.10
  1.7 0.0 copy-start.1
  1.7 1.8 %copy-done.1 = bf16[16,360,256]{2,1,0:T(8,128)(2,1)S(1)} copy-done((bf16[16,360,256]{2,1,0:T(8,128)(2,1)S(1)}, bf16[16,360,256]{2,1,0:T(8,128)(2,1)}, u32[]{:S(2)}) %copy-start.1) | copy-done | bytes 2949144
  3.6 0.0 copy-start.3
  3.6 1.7 %copy-done.3 = bf16[4,768,360]{2,1,0:T(8,128)(2,1)S(1)} copy-done((bf16[4,768,360]{2,1,0:T(8,128)(2,1)S(1)}, bf16[4,768,360]{2,1,0:T(8,128)(2,1)}, u32[]{:S(2)}) %copy-start.3) | copy-done | bytes 2211864
  5.2 62.3 %shard_map.64 = (bf16[32,4,24,256]{3,2,1,0:T(8,128)(2,1)S(1)}, bf16[8,12,16,192]{3,2,1,0:T(8,128)(2,1)S(1)}) custom-call(bf16[4,4,360,256]{3,2,1,0:T(8,128)(2,1)S(1)} %bitcast.33, bf16[8,12,16,192]{3,2,1,0:T(8,128)(2,1)S(1)} %bitcast.34, bf16[4,768,360]{2,1,0:T(8,128)(2,1)S(1)} %copy-done.3), custom_call_target="tpu_custom_call" | custom-call | tf_op jit(solution)/shard_map/pallas_call | solution.py:318
  67.6 0.1 select_bitcast_fusion
  67.6 0.1 copy.11
  67.7 0.4 convert_element_type.35
  68.1 0.4 add_convert_fusion.1
  68.5 0.4 copy.12
  68.9 0.2 add.47
  69.1 0.4 copy.13
  69.5 0.2 sub.25
  69.7 3.6 %convolution_convert_fusion = bf16[2,12,192,2,256]{4,2,3,1,0:T(8,128)(2,1)} fusion(bf16[2,12,64,192,1]{3,2,4,1,0:T(8,128)(2,1)S(1)} %bitcast.36, bf16[1,64,2,12,256]{4,1,3,2,0:T(8,128)(2,1)S(1)} %sub.25, bf16[1,64,2,12,256]{4,1,3,2,0:T(8,128)(2,1)S(1)} %add.47), kind=kOutput, calls=%fused_computation.7 | convolution fusion | flops 305135616 | bytes 6881280 | tf_op jit(solution)/shard_map/qmrk,qrpmc->qmkpc/dot_general | solution.py:409
  73.3 0.0 copy-start.5
  73.3 9.4 %copy.23 = bf16[2,12,192,2,256]{4,3,2,1,0:T(2,128)(2,1)} copy(bf16[2,12,192,2,256]{4,2,3,1,0:T(8,128)(2,1)} %convolution_convert_fusion) | data formatting | bytes 9437184
  82.7 0.0 copy-done.5
  82.7 6.5 %convert_bitcast_fusion = f32[2,64,2,12,256]{4,1,2,3,0:T(8,128)} fusion(bf16[2,12,64,192,1]{3,2,4,1,0:T(8,128)(2,1)S(1)} %bitcast.37, bf16[2,12,192,2,256]{4,3,2,1,0:T(2,128)(2,1)} %copy.23, bf16[256,256]{1,0:T(8,128)(2,1)S(1)} %copy-done.5), kind=kOutput, calls=%fused_computation.6 | convolution fusion | flops 1513881600 | bytes 8585216 | tf_op jit(solution)/shard_map/qmrk,qmkpc->qrpmc/dot_general | solution.py:415
  89.3 2.3 %add_convert_fusion = (bf16[1,64,2,12,256]{4,1,2,3,0:T(8,128)(2,1)S(1)}, bf16[1,64,2,12,256]{4,1,2,3,0:T(8,128)(2,1)S(1)}) fusion(f32[2,64,2,12,256]{4,1,2,3,0:T(8,128)} %convert_bitcast_fusion), kind=kLoop, calls=%fused_computation.13 | loop fusion | flops 1572864 | bytes 4718592 | tf_op jit(solution)/shard_map/convert.2 | solution.py:444
  91.6 0.1 pad_maximum_fusion.1
  91.7 2.5 %copy.21 = bf16[2,64,2,12,256]{4,3,2,1,0:T(8,128)(2,1)} copy(bf16[2,64,2,12,256]{4,1,2,3,0:T(8,128)(2,1)S(1)} %pad_maximum_fusion.1) | data formatting | bytes 3145728 | tf_op jit(solution)/shard_map/convert_element_type | solution.py:419
  94.2 2.5 %reshape.52.grads_ref = bf16[32,4,24,256]{3,2,1,0:T(8,128)(2,1)S(1)} reshape(bf16[2,64,2,12,256]{4,3,2,1,0:T(8,128)(2,1)} %copy.21) | data formatting | bytes 3145728 | tf_op jit(solution)/shard_map/convert_element_type | solution.py:419
  96.7 0.0 copy-start.4
  96.7 1.6 copy-done.4
  98.3 0.0 copy-start.2
  98.3 64.3 %shard_map.65 = bf16[4,4,360,256]{3,2,1,0:T(8,128)(2,1)S(1)} custom-call(bf16[32,4,24,256]{3,2,1,0:T(8,128)(2,1)S(1)} %reshape.52.grads_ref, bf16[4,360,768]{2,1,0:T(8,128)(2,1)S(1)} %copy-done.4), custom_call_target="tpu_custom_call" | custom-call | tf_op jit(solution)/shard_map/pallas_call | solution.py:350
  162.7 0.0 copy-done
  162.7 0.0 copy-done.2
  162.7 2.6 %fusion = bf16[16,360,256]{2,1,0:T(8,128)(2,1)} fusion(bf16[4,4,360,256]{3,2,1,0:T(8,128)(2,1)S(1)} %shard_map.65, bf16[16,360,256]{2,1,0:T(8,128)(2,1)S(1)} %copy-done.2, bf16[256,256]{1,0:T(8,128)(2,1)S(1)} %copy-done), kind=kOutput, calls=%fused_computation.1 | convolution fusion | flops 759398400 | bytes 8978432 | tf_op jit(solution)/shard_map/dot_general | solution.py:431
  (5 shorter events, 0.0 us)
Async XLA Ops:
  0.0 162.7 %copy-start = (bf16[256,256]{1,0:T(8,128)(2,1)S(1)}, bf16[256,256]{1,0:T(8,128)(2,1)}, u32[]{:S(2)}) copy-start(bf16[256,256]{1,0:T(8,128)(2,1)} %param.9) | copy-start | bytes 393220
  1.7 1.8 %copy-start.1 = (bf16[16,360,256]{2,1,0:T(8,128)(2,1)S(1)}, bf16[16,360,256]{2,1,0:T(8,128)(2,1)}, u32[]{:S(2)}) copy-start(bf16[16,360,256]{2,1,0:T(8,128)(2,1)} %param.6) | copy-start | bytes 8847364
  3.6 1.7 %copy-start.3 = (bf16[4,768,360]{2,1,0:T(8,128)(2,1)S(1)}, bf16[4,768,360]{2,1,0:T(8,128)(2,1)}, u32[]{:S(2)}) copy-start(bf16[4,768,360]{2,1,0:T(8,128)(2,1)} %constant.38.clone.table_ref) | copy-start | bytes 6635524
  73.3 9.4 %copy-start.5 = (bf16[256,256]{1,0:T(8,128)(2,1)S(1)}, bf16[256,256]{1,0:T(8,128)(2,1)}, u32[]{:S(2)}) copy-start(bf16[256,256]{1,0:T(8,128)(2,1)} %param.8) | copy-start | bytes 393220
  96.7 1.6 copy-start.4
  98.3 64.4 %copy-start.2 = (bf16[16,360,256]{2,1,0:T(8,128)(2,1)S(1)}, bf16[16,360,256]{2,1,0:T(8,128)(2,1)}, u32[]{:S(2)}) copy-start(bf16[16,360,256]{2,1,0:T(8,128)(2,1)} %param.6) | copy-start | bytes 8847364
